TPU v7x, 512 devices: a whole 4x4x16 slice. The times are simulated.
512 devices in a mesh: ev: 16 (over y_hi, x, core), cuts: 32 (over z, y_lo).
Axes of the slice: x: 4, y: 4 (y_hi: 2, y_lo: 2; y = y_hi * 2 + y_lo), z: 16, core: 2. Of those that a mesh axis runs over, the one named last changes fastest.
Arguments:
- kernels: float32 [16, 3, 32, 262144], P('ev', None, 'cuts')
- coords: float32 [3, 32, 262144], P(None, 'cuts', 'ev')
- neighbours: int32 [32, 2048, 9], P('cuts', 'ev'), may hold values from -1 to 389, as said below
Outputs:
- smoothed: float32 [3, 32, 262144], P(None, 'cuts', 'ev')
- irls_weights: float32 [3, 32, 262144], P(None, 'cuts', 'ev')
Inputs may be any that keep to these rules, and one draw needn't show every extreme that they name: `neighbours`: each tile's nine slots name tiles among the 3 by (130) block around its device's tiles (the same and the two neighbouring slices, one tile beyond each end of the device's run), padded with -1; the tile's own slot (slot 4) is never -1 and no slot names a tile outside the mesh.
All inputs are finite; a program needn't handle non-finite values.
Results may differ from a plain program's by a relative error of at most 0.0003.
Values sent between devices are 32-bit elements; how exact they have to be, the bound alone decides.
A program may use at most 64 MiB of HBM per device.

v0:
```python
import jax
import jax.numpy as jnp
from jax import lax
from jax.sharding import PartitionSpec as P


def extended(cells, sides, width):
    for axis, dim in sides:
        count = lax.axis_size(axis)
        ends = count - 1
        head = lax.slice_in_dim(cells, 0, width, axis=dim)
        tail = lax.slice_in_dim(cells, cells.shape[dim] - width, cells.shape[dim], axis=dim)
        cells = jnp.concatenate(
            [
                lax.ppermute(tail, axis, [(i, (i + 1) % count) for i in range(ends)]),
                cells,
                lax.ppermute(head, axis, [((i + 1) % count, i) for i in range(ends)]),
            ],
            axis=dim,
        )
    return cells


def smooth_block(own_x, grid, ids):
    count = grid.shape[0] - 3
    tiles = ids.shape[0]
    group = 4
    xs = jnp.transpose(own_x.reshape(3, tiles // group, group, 128), (1, 0, 2, 3))
    ids_grouped = ids.reshape(tiles // group, group, ids.shape[1])

    def one(pair):
        here, idx = pair
        safe = jnp.maximum(idx, 0)
        valid = (idx >= 0).astype(jnp.float32)
        near = jnp.take(grid, safe.reshape(-1), axis=1).reshape(
            grid.shape[0], group, idx.shape[1], 128
        )
        dist = jnp.zeros((group, 128, idx.shape[1], 128), jnp.float32)
        for axis_id in range(3):
            diff = here[axis_id][:, :, None, None] - near[count + axis_id][:, None, :, :]
            dist = dist + diff * diff
        weights = jnp.exp(dist * (-1.0 / 0.72)) * valid[:, None, :, None]
        numer = jnp.einsum("tpsq,ktsq->ktp", weights, near[:count], precision=lax.Precision.HIGHEST)
        denom = jnp.sum(weights, axis=(2, 3))
        return numer / denom[None]

    out = lax.map(one, (xs, ids_grouped))
    return jnp.transpose(out, (1, 0, 2, 3)).reshape(out.shape[1], tiles, 128)


def on_device(kernels, coords, neighbours):
    local = kernels[0]
    total = lax.psum(local, "ev")
    width = total.shape[2] // lax.axis_size("ev")
    owned = lax.dynamic_slice_in_dim(total, lax.axis_index("ev") * width, width, 2)
    count = owned.shape[0]
    points = owned.shape[2]
    tiles = points // 128
    stacked = jnp.concatenate([owned, coords], axis=0).reshape(count + 3, 1, tiles, 128)
    padded = extended(stacked, (("ev", 2), ("cuts", 1)), 1)
    grid = padded.reshape(count + 3, 3 * (tiles + 2), 128)
    own_x = coords.reshape(3, tiles, 128)
    smoothed = smooth_block(own_x, grid, neighbours[0]).reshape(count, 1, points)
    spread = jnp.sqrt(smoothed * smoothed + 0.01)
    lp_sum = lax.psum(jnp.sum(spread), ("ev", "cuts"))
    everything = count * points * lax.axis_size("ev") * lax.axis_size("cuts")
    irls_weights = lp_sum / everything / spread
    return (smoothed, irls_weights)


def solution(mesh):
    placed = (P("ev", None, "cuts", None), P(None, "cuts", "ev"), P("cuts", "ev", None))
    return jax.shard_map(
        on_device,
        mesh=mesh,
        in_specs=placed,
        out_specs=(P(None, "cuts", "ev"), P(None, "cuts", "ev")),
        check_vma=False,
    )
```

profile of v0, /device:TPU:1, one launch (start us, length us, event | category | flops | bytes accessed | tf_op | source)
XLA Modules:
  0.0 504.3 jit_solution(9763959306523700627)
XLA Ops:
  7.9 170.5 %all-reduce.2.cloned.1.call-done = f32[3,1,262144]{2,1,0:T(1,128)} async-done(((f32[3,1,262144]{2,1,0:T(1,128)}), f32[3,1,262144]{2,1,0:T(1,128)}) %all-reduce.2.cloned.1.call-update) | async-done | bytes 3145744 | tf_op jit(solution)/shard_map/psum | solution.py:53
  190.7 15.5 %collective-permute-done.2 = f32[6,1,130,128]{3,1,2,0:T(1,128)S(1)} collective-permute-done((f32[6,1,130,128]{3,1,2,0:T(1,128)S(1)}, f32[6,1,130,128]{3,1,2,0:T(1,128)S(1)}, u32[]{:S(2)}, u32[]{:S(2)}) %collective-permute-start.2) | collective-permute-done | bytes 399392 | tf_op jit(solution)/shard_map/ppermute | solution.py:15
  207.6 178.9 %while.10 = (s32[]{:T(128)}, f32[32,3,4,128]{3,1,2,0:T(4,128)S(1)}, s32[32,4,9]{2,1,0:T(4,128)S(1)}, f32[6,390,128]{2,0,1:T(8,128)S(1)}, f32[32,3,4,128]{3,2,0,1:T(4,128)S(1)}, /*index=5*/s32[]{:T(128)}) while((s32[]{:T(128)}, f32[32,3,4,128]{3,1,2,0:T(4,128)S(1)}, s32[32,4,9]{2,1,0:T(4,128)S(1)}, f32[6,390,128]{2,0,1:T(8,128)S(1)}, ...), condition=%wide.region_3.4_spmd, body=%wide.region_1.3_spmd.sunk | while | flops 33649808 | bytes 1058145 | solution.py:47
  210.1 3.1 fusion.22
  215.7 3.1 fusion.22
  221.3 3.1 fusion.22
  226.9 3.1 fusion.22
  232.5 3.1 fusion.22
  238.1 3.1 fusion.22
  243.7 3.1 fusion.22
  249.3 3.1 fusion.22
  254.9 3.1 fusion.22
  260.5 3.1 fusion.22
  266.0 3.1 fusion.22
  271.6 3.1 fusion.22
  277.2 3.1 fusion.22
  282.8 3.1 fusion.22
  288.4 3.1 fusion.22
  299.6 3.1 fusion.22
  305.2 3.1 fusion.22
  310.8 3.1 fusion.22
  316.4 3.1 fusion.22
  322.0 3.1 fusion.22
  387.4 108.5 %psum.15 = f32[]{:T(128)} all-reduce(f32[]{:T(128)} %sqrt_reduce_fusion), channel_id=1, replica_groups=mesh['ev'=16,'cuts'=32] {'ev','cuts'}, use_global_device_ids=true, to_apply=%region_5.6 | all-reduce | flops 1 | bytes 8 | tf_op jit(solution)/shard_map/psum | solution.py:65
  (486 shorter events, 130.9 us)
Async XLA Ops:
  7.2 172.2 %copy-start.1 = (f32[3,1,16384]{2,1,0:T(1,128)S(1)}, f32[3,1,16384]{2,1,0:T(1,128)}, u32[]{:S(2)}) copy-start(f32[3,1,16384]{2,1,0:T(1,128)} %param.6) | copy-start | bytes 589828
  7.2 171.3 %all-reduce.2.cloned.1.call-start = ((), (), s32[]{:S(2)}) async-start(), calls=%async_computation | async-start | bytes 6291456 | tf_op jit(solution)/shard_map/psum | solution.py:53
  7.2 183.3 %copy-start.2 = (s32[1,128,9]{1,0,2:T(1,128)S(1)}, s32[1,128,9]{1,0,2:T(1,128)}, u32[]{:S(2)}) copy-start(s32[1,128,9]{1,0,2:T(1,128)} %param.7) | copy-start | bytes 13828
  179.8 4.7 collective-permute-start
  181.7 4.9 collective-permute-start.1
  187.0 19.2 %collective-permute-start.2 = (f32[6,1,130,128]{3,1,2,0:T(1,128)S(1)}, f32[6,1,130,128]{3,1,2,0:T(1,128)S(1)}, u32[]{:S(2)}, u32[]{:S(2)}) collective-permute-start(f32[6,1,130,128]{3,1,2,0:T(1,128)S(1)} %pad_maximum_fusion.1), channel_id=1, source_target_pairs={{0,1},{1,2},{2,3},{3,4},{4,5},{5,6},{6,7},{7,8},{8,9},{9,10},{10,1... | collective-permute-start | bytes 1198088 | tf_op jit(solution)/shard_map/ppermute | solution.py:15
  189.3 16.9 %collective-permute-start.3 = (f32[6,1,130,128]{3,1,2,0:T(1,128)S(1)}, f32[6,1,130,128]{3,1,2,0:T(1,128)S(1)}, u32[]{:S(2)}, u32[]{:S(2)}) collective-permute-start(f32[6,1,130,128]{3,1,2,0:T(1,128)S(1)} %pad_maximum_fusion.1), channel_id=1, source_target_pairs={{1,0},{2,1},{3,2},{4,3},{5,4},{6,5},{7,6},{8,7},{9,8},{10,9},{11,1... | collective-permute-start | bytes 1198088 | tf_op jit(solution)/shard_map/ppermute | solution.py:17
  387.4 110.1 %copy-start = (f32[3,32,4,128]{3,2,1,0:T(4,128)}, f32[3,32,4,128]{3,2,1,0:T(4,128)S(1)}, u32[]{:S(2)}) copy-start(f32[3,32,4,128]{3,2,1,0:T(4,128)S(1)} %copy.24) | copy-start | bytes 589828
Sparse Core Ops, SparseCore 0:
  11.0 167.4 all-reduce.1
where the time goes:
time: 505 us; the launch traced here: 504 us
  waiting for transfers between devices  189 us (37%)
  blocking collectives  109 us (22%)
  matrix products  98.3 us (19%)
  other arithmetic  50.9 us (10%)
  local copies, waits for them, and re-layouts  32.1 us (6%)
  between operations  14.8 us (3%)
  starting transfers between devices  8.24 us (2%)
    psum x1, waiting for transfers between devices, on_device(): total = lax.psum(local, 'ev')  171 us
    psum x1, blocking collectives, on_device(): lp_sum = lax.psum(jnp.sum(spread), ('ev', 'cuts'))  109 us
    dot_general x32, matrix products, one(): jnp.einsum('tpsq,ktsq->ktp', weights, near[:count], precision=lax.Precisi...  98.3 us
    reduce_sum x32, other arithmetic, one(): denom = jnp.sum(weights, axis=(2, 3))  43.3 us
    gather x32, local copies, waits for them, and re-layouts, one(): jnp.take(grid, safe.reshape(-1), axis=1)  19 us
    ppermute x2, waiting for transfers between devices, extended(): lax.ppermute(tail, axis, [(i, (i + 1) % count) for i in range(ends)])  15.5 us
  transfers between devices with their start and end apart: 5, of which 3 were waited for; matrix products, arithmetic and copies ran while one was open for 0% of the time, Pallas kernels for 0%

commit v1 on v0

v1 whole, which is shorter than its diff:
```python
import functools
import jax
import jax.numpy as jnp
from jax import lax
from jax.experimental import pallas as pl
from jax.experimental.pallas import tpu as pltpu
from jax.sharding import PartitionSpec as P

MESH = pl.DeviceIdType.MESH
f32 = jnp.float32


def exchange(pieces, with_halo, cuts, d, x_ref, vg, xg, vcorner, xcorner,
             mine, other, x1, x2, yb, loc_sem, s0, r0, s1, r1, s2, r2, s3, r3, sh, rh):
    ev = lax.axis_index("ev")
    cut = lax.axis_index("cuts")
    core = lax.rem(ev, 2)
    x = lax.rem(lax.div(ev, 2), 4)
    yh = lax.div(ev, 8)

    def at(y_, x_, c_):
        return (y_ * 8 + x_ * 2 + c_, cut)

    xp, xm, xo = lax.rem(x + 1, 4), lax.rem(x + 3, 4), lax.rem(x + 2, 4)
    twin = at(yh, x, 1 - core)
    right, left = at(yh, xp, core), at(yh, xm, core)
    across = at(1 - yh, x, core)

    rel = [(0, -1), (0, 1)] + [(de, dc) for de in (-1, 1) for dc in (-1, 0, 1)] if with_halo else []

    def exists(de, dc):
        ok = jnp.bool_(True)
        if de: ok = ok & (ev + de >= 0) & (ev + de < 16)
        if dc: ok = ok & (cut + dc >= 0) & (cut + dc < cuts)
        return ok

    barrier = pltpu.get_barrier_semaphore()
    for dev in (twin, right, left, across):
        pl.semaphore_signal(barrier, inc=1, device_id=dev, device_id_type=MESH)
    for de, dc in rel:
        @pl.when(exists(de, dc))
        def _(de=de, dc=dc):
            pl.semaphore_signal(barrier, inc=1, device_id=(ev + de, cut + dc), device_id_type=MESH)
    expect = 4
    for de, dc in rel:
        expect = expect + exists(de, dc).astype(jnp.int32)

    n = len(pieces)
    width = [b - a for a, b in pieces]
    rows = [pl.ds(a, b - a) for a, b in pieces]
    ha = [pl.ds(a, (b - a) // 2) for a, b in pieces]
    hb = [pl.ds(a + (b - a) // 2, (b - a) // 2) for a, b in pieces]

    locs = []
    for p in range(n):
        c = pltpu.make_async_copy(d.at[:, :, :, core, rows[p]], mine.at[:, :, :, rows[p]], loc_sem.at[p])
        c.start()
        locs.append(c)
    pl.semaphore_wait(barrier, expect)

    def remote(src, dst, ss, rs, dev):
        c = pltpu.make_async_remote_copy(src_ref=src, dst_ref=dst, send_sem=ss, recv_sem=rs,
                                         device_id=dev, device_id_type=MESH)
        c.start()
        return c

    def halo(src, full, corner, base):
        for i, (de, dc) in enumerate(rel):
            if de == 0:
                s, t = src, full.at[1 - dc]
            else:
                s = src.at[:, pl.ds(120 if de > 0 else 0, 8)]
                t = corner.at[1 - dc, 0 if de > 0 else 1]
            c = pltpu.make_async_remote_copy(src_ref=s, dst_ref=t, send_sem=sh.at[base + i], recv_sem=rh.at[base + i],
                                             device_id=(ev + de, cut + dc), device_id_type=MESH)
            pl.when(exists(de, dc))(c.start)

    def halo_wait(src, full, corner, base):
        for i, (de, dc) in enumerate(rel):
            if de == 0:
                s, t = src, full.at[1 - dc]
            else:
                s = src.at[:, pl.ds(120 if de > 0 else 0, 8)]
                t = corner.at[1 - dc, 0 if de > 0 else 1]
            c = pltpu.make_async_remote_copy(src_ref=s, dst_ref=t, send_sem=sh.at[base + i], recv_sem=rh.at[base + i],
                                             device_id=(ev + de, cut + dc), device_id_type=MESH)
            pl.when(exists(de, dc))(c.wait_send)
            pl.when(exists(-de, -dc))(c.wait_recv)

    order = [xo, xp, xm, x]
    c0 = {}
    for p in range(n):
        for i, xx in enumerate(order):
            c0[p, i] = remote(d.at[:, :, xx, 1 - core, rows[p]], other.at[:, :, xx, rows[p]],
                              s0.at[p * 4 + i], r0.at[p * 4 + i], twin)
    if with_halo:
        halo(x_ref, xg, xcorner, 8)
    c1 = {}
    for p in range(n):
        locs[p].wait()
        c0[p, 0].wait_recv()
        mine[:, :, xo, rows[p]] += other[:, :, xo, rows[p]]
        c1[p, 0] = remote(mine.at[:, :, xo, ha[p]], x1.at[0, :, :, pl.ds(pieces[p][0] // 2, width[p] // 2)],
                          s1.at[2 * p], r1.at[2 * p], right)
        c1[p, 1] = remote(mine.at[:, :, xo, hb[p]], x1.at[1, :, :, pl.ds(pieces[p][0] // 2, width[p] // 2)],
                          s1.at[2 * p + 1], r1.at[2 * p + 1], left)
    c2 = {}
    for p in range(n):
        for side, xx, half in ((0, xp, ha[p]), (1, xm, hb[p])):
            c0[p, 1 + side].wait_recv()
            mine[:, :, xx, rows[p]] += other[:, :, xx, rows[p]]
            c1[p, side].wait_recv()
            mine[:, :, xx, half] += x1[side, :, :, pl.ds(pieces[p][0] // 2, width[p] // 2)]
            c2[p, side] = remote(mine.at[:, :, xx, rows[p]], x2.at[side, :, :, rows[p]],
                                 s2.at[2 * p + side], r2.at[2 * p + side], right if side == 0 else left)
    c3 = {}
    for p in range(n):
        c0[p, 3].wait_recv()
        mine[:, :, x, rows[p]] += other[:, :, x, rows[p]]
        for side in (0, 1):
            c2[p, side].wait_recv()
            mine[:, :, x, rows[p]] += x2[side, :, :, rows[p]]
        c3[p] = remote(mine.at[:, 1 - yh, x, rows[p]], yb.at[:, rows[p]], s3.at[p], r3.at[p], across)
    for p in range(n):
        c3[p].wait_recv()
        vg[1, :, rows[p]] = mine[:, yh, x, rows[p]] + yb[:, rows[p]]
    if with_halo:
        halo(vg.at[1], vg, vcorner, 0)
        xg[1] = x_ref[...]
    for c in c0.values(): c.wait_send()
    for c in c1.values(): c.wait_send()
    for c in c2.values(): c.wait_send()
    for c in c3.values(): c.wait_send()
    if with_halo:
        halo_wait(x_ref, xg, xcorner, 8)
        halo_wait(vg.at[1], vg, vcorner, 0)


def run_exchange(kern, coords, cuts, pieces, with_halo=True):
    n = len(pieces)
    vm = pl.BlockSpec(memory_space=pltpu.VMEM)
    dma = pltpu.SemaphoreType.DMA
    return pl.pallas_call(
        functools.partial(exchange, pieces, with_halo, cuts),
        out_shape=[jax.ShapeDtypeStruct((3, 3, 128, 128), f32)] * 2 + [jax.ShapeDtypeStruct((3, 2, 3, 8, 128), f32)] * 2,
        in_specs=[pl.BlockSpec(memory_space=pl.ANY), vm],
        out_specs=[vm] * 4,
        scratch_shapes=[
            pltpu.VMEM((3, 2, 4, 128, 128), f32), pltpu.VMEM((3, 2, 4, 128, 128), f32),
            pltpu.VMEM((2, 3, 2, 64, 128), f32), pltpu.VMEM((2, 3, 2, 128, 128), f32),
            pltpu.VMEM((3, 128, 128), f32),
            dma((n,)), dma((4 * n,)), dma((4 * n,)), dma((2 * n,)), dma((2 * n,)), dma((2 * n,)), dma((2 * n,)),
            dma((n,)), dma((n,)), dma((16,)), dma((16,))],
        compiler_params=pltpu.CompilerParams(collective_id=0, has_side_effects=True, vmem_limit_bytes=40 * 2**20),
        name="event_sum_and_halo",
    )(kern, coords)
C2 = 1.4426950408889634 / 0.72
CLASSES = (9, 8, 7, 6, 5, 4)
ZERO = 391
LIMIT = 1.5
SHIFT = C2 * 3.0 * LIMIT * LIMIT
NT = (((1,), (1,)), ((), ()))
bf16 = jnp.bfloat16


def plan_slots(ids):
    tiles = ids.shape[0]
    valid = ids >= 0
    safe = jnp.maximum(ids, 0)
    row, col = safe // 130, safe % 130
    spot = jnp.where(col == 0, 384 + 2 * row, jnp.where(col == 129, 385 + 2 * row, row * 128 + col - 1))
    rank = jnp.cumsum(valid, axis=1) - 1
    j = jnp.arange(9)
    hit = (rank[:, None, :] == j[None, :, None]) & valid[:, None, :]
    named = jnp.sum(jnp.where(hit, spot[:, None, :], 0), axis=2) + jnp.where(jnp.any(hit, axis=2), 0, ZERO)
    named = jnp.concatenate([named, jnp.full((8, 9), ZERO)], axis=0)
    size = jnp.maximum(jnp.sum(valid, axis=1), CLASSES[-1])
    member = size[:, None] == jnp.array(CLASSES)[None, :]
    counts = jnp.sum(member, axis=0)
    pairs = (counts + 1) // 2
    start = 2 * (jnp.cumsum(pairs) - pairs)
    within = jnp.cumsum(member, axis=0) - 1
    place = jnp.sum(jnp.where(member, start[None, :] + within, 0), axis=1)
    slots = jnp.arange(144)
    found = place[None, :] == slots[:, None]
    order = jnp.sum(jnp.where(found, jnp.arange(tiles)[None, :], 0), axis=1) + jnp.where(jnp.any(found, axis=1), 0, tiles)
    i32 = jnp.int32
    return order.astype(i32), jnp.concatenate([start, pairs]).astype(i32), named.reshape(-1).astype(i32)


def smooth_kernel(order, spans, named, vg, xg, vc, xc, out, lp, vtab, xtab, ctab, sm, ha, hb, pa, pb, ra, rb):
    vtab[...] = jnp.zeros_like(vtab)
    row8 = lax.broadcasted_iota(jnp.int32, (1, 8, 128), 1)

    def three(a, b, c):
        n = a.shape[0]
        wide = lambda r: jnp.broadcast_to(r[:, None, :], (n, 8, 128))
        return jnp.where(row8 == 0, wide(a), jnp.where(row8 == 1, wide(b), wide(c)))

    def values(at, v):
        n = v.shape[0]
        v = jnp.where(row8 < 3, v, jnp.where(row8 == 3, 1.0, 0.0))
        hi = v.astype(bf16).astype(f32)
        vtab[at:at + n] = jnp.concatenate([hi, v - hi], axis=1).astype(bf16)

    for s in range(3):
        for g in range(0, 128, 32):
            at = s * 128 + g
            xtab[at:at + 32] = three(*[xg[s, k, g:g + 32] for k in range(3)])
            values(at, three(*[vg[s, k, g:g + 32] for k in range(3)]))
        for e, r in ((0, 7), (1, 0)):
            at = 384 + 2 * s + e
            xtab[at:at + 1] = three(*[xc[s, e, k, r:r + 1] for k in range(3)])
            values(at, three(*[vc[s, e, k, r:r + 1] for k in range(3)]))
    xtab[390:] = jnp.zeros((10, 8, 128), f32)
    own = xg[1]
    low, high = jnp.min(own, axis=2, keepdims=True), jnp.max(own, axis=2, keepdims=True)
    reach = jnp.max(0.5 * high - 0.5 * low)
    mid = jnp.broadcast_to(0.5 * high + 0.5 * low, own.shape)
    for g in range(0, 128, 32):
        ctab[g:g + 32] = three(*[mid[k, g:g + 32] for k in range(3)])
    ctab[128:] = jnp.zeros((8, 8, 128), f32)

    def columns(rows, px):
        for a in range(3):
            px[a] = jnp.transpose(jnp.broadcast_to(rows[a:a + 1], (128, 128)))

    def prepare(n, t, px, rows):
        c = ctab[t]
        columns(xtab[128 + t] - c, px)
        for s in range(n):
            y = jnp.clip(xtab[named[t * 9 + s]] - c, -1e4, 1e4)
            b = y * y
            rows[s] = y * (2 * C2)
            rows[s, 3:4] = (b[0:1] + b[1:2] + b[2:3]) * (-C2) - SHIFT

    def weigh(n, px, rows, h):
        for p in range(0, 128, 32):
            cols = [px[a, p:p + 32] for a in range(3)]
            for s in range(n):
                r = [jnp.broadcast_to(rows[s, k:k + 1], (32, 128)) for k in range(4)]
                w = jnp.exp2(((cols[0] * r[0] + r[3]) + cols[1] * r[1]) + cols[2] * r[2])
                hi = w.astype(bf16)
                h[p:p + 32, s * 128:(s + 1) * 128] = hi
                h[128 + p:160 + p, s * 128:(s + 1) * 128] = (w - hi.astype(f32)).astype(bf16)

    def settle(t, r):
        total = r[:, :128] + r[:, 128:]
        mean = (total[0:3] + total[8:11]) / total[3:4]
        for k in range(3):
            sm[k, pl.ds(t, 1)] = mean[k:k + 1]

    def gather(n, t, h):
        v = jnp.concatenate([vtab[named[t * 9 + s]] for s in range(n)], axis=1)
        settle(t, lax.dot_general(v, h[:, :n * 128], NT, preferred_element_type=f32))

    @pl.when(reach <= LIMIT)
    def _():
        for c, n in enumerate(CLASSES):
            first, pairs = spans[c], spans[len(CLASSES) + c]

            @pl.when(pairs > 0)
            def _(n=n, first=first, pairs=pairs):
                prepare(n, order[first], pa, ra)

                def body(i, _):
                    at = first + 2 * i
                    t, u, nxt = order[at], order[at + 1], order[at + 2]
                    before = jnp.where(i == 0, 128, order[jnp.maximum(at - 1, 0)])
                    prepare(n, u, pb, rb)
                    gather(n, before, hb)
                    weigh(n, pa, ra, ha)
                    prepare(n, nxt, pa, ra)
                    gather(n, t, ha)
                    weigh(n, pb, rb, hb)
                    return 0

                lax.fori_loop(0, pairs, body, 0)
                gather(n, order[first + 2 * pairs - 1], hb)

    @pl.when(jnp.logical_not(reach <= LIMIT))
    def _():
        def tile(t, _):
            columns(xtab[128 + t], pa)

            def slot(s, total):
                g = named[t * 9 + s]
                q = xtab[g]
                dist = jnp.zeros((128, 128), f32)
                for a in range(3):
                    diff = pa[a] - q[a:a + 1]
                    dist = dist + diff * diff
                w = jnp.exp(dist * (-1.0 / 0.72))
                hi = w.astype(bf16)
                both = jnp.concatenate([hi, (w - hi.astype(f32)).astype(bf16)], axis=0)
                return total + lax.dot_general(vtab[g], both, NT, preferred_element_type=f32)

            settle(t, lax.fori_loop(0, 9, slot, jnp.zeros((16, 256), f32)))
            return 0

        lax.fori_loop(0, 128, tile, 0)

    got = sm[:, 0:128]
    out[...] = got
    spread = jnp.sqrt(got * got + 0.01)
    lp[...] = jnp.sum(spread.reshape(48, 8, 128), axis=0)


def run_smooth(order, spans, named, vg, xg, vc, xc):
    vm, sm = pl.BlockSpec(memory_space=pltpu.VMEM), pl.BlockSpec(memory_space=pltpu.SMEM)
    return pl.pallas_call(
        smooth_kernel,
        out_shape=[jax.ShapeDtypeStruct((3, 128, 128), f32), jax.ShapeDtypeStruct((8, 128), f32)],
        in_specs=[sm] * 3 + [vm] * 4,
        out_specs=[vm] * 2,
        scratch_shapes=[
            pltpu.VMEM((400, 16, 128), bf16), pltpu.VMEM((400, 8, 128), f32), pltpu.VMEM((136, 8, 128), f32),
            pltpu.VMEM((3, 136, 128), f32),
            pltpu.VMEM((256, 1152), bf16), pltpu.VMEM((256, 1152), bf16),
            pltpu.VMEM((3, 128, 128), f32), pltpu.VMEM((3, 128, 128), f32),
            pltpu.VMEM((9, 8, 128), f32), pltpu.VMEM((9, 8, 128), f32)],
        compiler_params=pltpu.CompilerParams(vmem_limit_bytes=40 * 2**20),
        name="smooth_tiles",
    )(order, spans, named, vg, xg, vc, xc)


def total_kernel(cuts, part, out, held, ss, rs):
    ev, cut = lax.axis_index("ev"), lax.axis_index("cuts")
    steps = []
    lows = 8 if cuts % 8 == 0 else cuts
    high = cuts // lows
    steps.append([(lax.rem(ev + d, 16), cut) for d in range(1, 16)])
    base, lane = lax.div(cut, lows) * lows, lax.rem(cut, lows)
    steps.append([(ev, base + lax.rem(lane + d, lows)) for d in range(1, lows)])
    if high > 1:
        steps.append([(ev, lax.rem(cut + d * lows, cuts)) for d in range(1, high)])
    barrier = pltpu.get_barrier_semaphore()
    n = 0
    for step in steps:
        for dev in step:
            pl.semaphore_signal(barrier, inc=1, device_id=dev, device_id_type=MESH)
            n += 1
    here = jnp.sum(part[...], axis=(0, 1), keepdims=True)
    held[0] = jnp.broadcast_to(here, (8, 128))
    pl.semaphore_wait(barrier, n)
    slot, mine, sem = 1, 0, 0
    for step in steps:
        copies = []
        for d, dev in enumerate(step):
            c = pltpu.make_async_remote_copy(src_ref=held.at[mine], dst_ref=held.at[slot + d], send_sem=ss.at[sem], recv_sem=rs.at[sem],
                                             device_id=dev, device_id_type=MESH)
            c.start()
            copies.append(c)
            sem += 1
        total = held[mine]
        for d, c in enumerate(copies):
            c.wait_recv()
            total = total + held[slot + d]
        for c in copies:
            c.wait_send()
        slot += len(step)
        mine = slot
        held[mine] = total
        slot += 1
    out[...] = held[mine]


def run_total(part, cuts):
    vm = pl.BlockSpec(memory_space=pltpu.VMEM)
    dma = pltpu.SemaphoreType.DMA
    return pl.pallas_call(
        functools.partial(total_kernel, cuts),
        out_shape=jax.ShapeDtypeStruct((8, 128), f32),
        in_specs=[vm], out_specs=vm,
        scratch_shapes=[pltpu.VMEM((64, 8, 128), f32), dma((48,)), dma((48,))],
        compiler_params=pltpu.CompilerParams(collective_id=1, has_side_effects=True),
        name="sum_over_devices",
    )(part)


def on_device(cuts, kernels, coords, neighbours):
    pieces = [(0, 64), (64, 128)]
    plan = plan_slots(neighbours[0])
    vg, xg, vc, xc = run_exchange(kernels.reshape(3, 2, 4, 2, 128, 128), coords.reshape(3, 128, 128), cuts, pieces)
    smoothed, part = run_smooth(*plan, vg, xg, vc, xc)
    total = run_total(part, cuts)[0, 0]
    smoothed = smoothed.reshape(3, 1, 16384)
    everything = 3 * 16384 * 16 * cuts
    return smoothed, total / everything / jnp.sqrt(smoothed * smoothed + 0.01)


def solution(mesh):
    cuts = mesh.shape["cuts"]
    return jax.shard_map(
        functools.partial(on_device, cuts),
        mesh=mesh,
        in_specs=(P("ev", None, "cuts", None), P(None, "cuts", "ev"), P("cuts", "ev", None)),
        out_specs=(P(None, "cuts", "ev"), P(None, "cuts", "ev")),
        check_vma=False,
    )
```

time: 505 us -> 116 us (0.23)
  waiting for transfers between devices: 189 us -> 0 us
  blocking collectives: 109 us -> 0 us
  Pallas kernels: 0 us -> 102 us
  matrix products: 98.3 us -> 0 us
  other arithmetic: 50.9 us -> 4.64 us
  local copies, waits for them, and re-layouts: 32.1 us -> 6.82 us
  between operations: 14.8 us -> 1.37 us
  starting transfers between devices: 8.24 us -> 0 us
    psum x1 -> x0, waiting for transfers between devices: 171 us -> none  [on_device(): total = lax.psum(local, 'ev')]
    psum x1 -> x0, blocking collectives: 109 us -> none  [on_device(): lp_sum = lax.psum(jnp.sum(spread), ('ev', 'cuts'))]
    pallas_call x0 -> x3, Pallas kernels: none -> 102 us  [the longest x1 38.5 us: run_total(): pl.pallas_call(functools.partial(total_kernel, cuts), out_shape=jax.Shape...]
    dot_general x32 -> x0, matrix products: 98.3 us -> none  [one(): jnp.einsum('tpsq,ktsq->ktp', weights, near[:count], precision=lax.Precisi...]
    reduce_sum x33 -> x5, other arithmetic: 44.1 us -> 1.75 us  [the longest x1 0.82 us: plan_slots(): place = jnp.sum(jnp.where(member, start[None, :] + within, 0), axis=1)]
    gather x32 -> x0, local copies, waits for them, and re-layouts: 19 us -> none  [one(): jnp.take(grid, safe.reshape(-1), axis=1)]
    ppermute x4 -> x0, waiting for transfers between devices: 17.6 us -> none  [the longest x2 15.5 us: extended(): lax.ppermute(tail, axis, [(i, (i + 1) % count) for i in range(ends)])]
    ppermute x4 -> x0, starting transfers between devices: 8.2 us -> none  [the longest x2 4.16 us: extended(): lax.ppermute(tail, axis, [(i, (i + 1) % count) for i in range(ends)])]
  transfers between devices with their start and end apart: 5 -> 0, of which waited for: 3 -> 0; matrix products, arithmetic and copies ran while one was open for 0% -> 0% of each run, Pallas kernels for 0% -> 0%
where the time goes in v1:
time: 116 us; the launch traced here: 115 us
  Pallas kernels  102 us (88%)
  local copies, waits for them, and re-layouts  6.82 us (6%)
  other arithmetic  4.64 us (4%)
  between operations  1.37 us (1%)
    pallas_call x1, Pallas kernels, run_total(): pl.pallas_call(functools.partial(total_kernel, cuts), out_shape=jax.Shape...  38.5 us
    pallas_call x1, Pallas kernels, run_exchange(): pl.pallas_call(functools.partial(exchange, pieces, with_halo, cuts), out_...  37 us
    pallas_call x1, Pallas kernels, run_smooth(): pl.pallas_call(smooth_kernel, out_shape=[jax.ShapeDtypeStruct((3, 128, 12...  26.7 us
    unnamed x8, local copies, waits for them, and re-layouts  4.39 us

profile of v1, /device:TPU:1, one launch (start us, length us, event | category | flops | bytes accessed | tf_op | source)
XLA Modules:
  0.0 115.0 jit_solution(18217978677883340792)
XLA Ops:
  0.6 0.7 fusion.18
  1.4 0.8 fusion.4
  2.1 0.2 reduce-window.7
  2.3 0.1 pad_add_fusion.spans
  2.4 0.7 select_select_fusion
  3.2 0.1 copy.33
  3.3 0.2 reshape.193.named
  3.5 0.7 compare_convert_fusion
  4.3 0.2 reduce_window_sum.29
  4.5 0.8 fusion.3
  5.3 0.1 fusion
  5.4 0.1 select_reduce_fusion.1
  5.6 0.0 copy-start
  5.6 1.9 %copy-done = f32[1,3,1,262144]{3,2,1,0:T(1,128)S(1)} copy-done((f32[1,3,1,262144]{3,2,1,0:T(1,128)S(1)}, f32[1,3,1,262144]{3,2,1,0:T(1,128)}, u32[]{:S(2)}) %copy-start) | copy-done | bytes 3145752
  7.4 0.0 copy-start.1
  7.4 0.9 copy-done.1
  8.4 37.0 %event_sum_and_halo.1 = (f32[3,3,128,128]{3,2,1,0:T(8,128)S(1)}, f32[3,3,128,128]{3,2,1,0:T(8,128)S(1)}, f32[3,2,3,8,128]{4,3,2,1,0:T(8,128)S(1)}, f32[3,2,3,8,128]{4,3,2,1,0:T(8,128)S(1)}) custom-call(f32[3,2,4,2,128,128]{5,4,3,2,1,0:T(8,128)S(1)} %bitcast.47, f32[3,128,128]{2,1,0:T(8,128)S(1)} %bitcast.48), custom_call_target="tpu_custom_call" | custom-call | tf_op jit(solution)/shard_map/event_sum_and_halo/pallas_call | solution.py:143
  45.3 26.7 %smooth_tiles.1 = (f32[3,128,128]{2,1,0:T(8,128)}, f32[8,128]{1,0:T(8,128)S(1)}) custom-call(s32[144]{0:T(256)S(1)} %select_add_fusion.1.order, s32[12]{0:T(128)S(1)} %pad_add_fusion.spans, s32[1224]{0:T(1024)S(1)} %reshape.193.named, f32[3,3,128,128]{3,2,1,0:T(8,128)S(1)} %get-tuple-element.8.vg, f32[3,3,128,128]{3,2,1,0:T(8,128)S(1)} %get-tuple-element.9.xg, ...), custom_call_target="tpu_custom_call" | custom-call | tf_op jit(solution)/shard_map/smooth_tiles/pallas_call | solution.py:311
  72.0 0.6 copy-done.2
  72.6 38.5 %sum_over_devices.1 = f32[8,128]{1,0:T(8,128)} custom-call(f32[8,128]{1,0:T(8,128)} %copy-done.2), custom_call_target="tpu_custom_call" | custom-call | tf_op jit(solution)/shard_map/sum_over_devices/pallas_call | solution.py:371
  111.1 1.2 %slice.3 = f32[1,1]{1,0:T(1,128)} slice(f32[8,128]{1,0:T(8,128)} %sum_over_devices.1), slice={[0:1], [0:1]} | slice | bytes 8 | tf_op jit(solution)/shard_map/slice | solution.py:386
  113.0 1.0 reshape.196
  114.0 0.1 rsqrt_multiply_fusion
  114.1 0.9 copy.32
  (11 shorter events, 0.2 us)
Async XLA Ops:
  5.6 1.9 %copy-start = (f32[1,3,1,262144]{3,2,1,0:T(1,128)S(1)}, f32[1,3,1,262144]{3,2,1,0:T(1,128)}, u32[]{:S(2)}) copy-start(f32[1,3,1,262144]{3,2,1,0:T(1,128)} %param.4) | copy-start | bytes 9437188
  7.4 0.9 copy-start.1
  72.0 0.6 copy-start.2

commit v2 on v0

v2 whole, which is shorter than its diff:
```python
import functools
import jax
import jax.numpy as jnp
from jax import lax
from jax.experimental import pallas as pl
from jax.experimental.pallas import tpu as pltpu
from jax.sharding import PartitionSpec as P

MESH = pl.DeviceIdType.MESH
f32 = jnp.float32
bf16 = jnp.bfloat16
C2 = 1.4426950408889634 / 0.72
CLASSES = (9, 8, 7, 6, 5)
PLACES = 144
ZERO = 391
LIMIT = 1.5
SHIFT = C2 * 3.0 * LIMIT * LIMIT
NT = (((1,), (1,)), ((), ()))
VM1, VM2 = 16, 12
PIECES = ((0, 48, True), (48, 96, True), (96, 128, False))


def three(a, b, c):
    n = a.shape[0]
    row = lax.broadcasted_iota(jnp.int32, (1, 8, 128), 1)
    wide = lambda r: jnp.broadcast_to(r[:, None, :], (n, 8, 128))
    return jnp.where(row == 0, wide(a), jnp.where(row == 1, wide(b), wide(c)))


def plan_slots(nb, plan, named, reach):
    i32 = jnp.int32
    zero = jnp.zeros((1, 128), i32)
    count = zero
    found = [zero + ZERO for _ in range(9)]
    for s in range(9):
        v = nb[s:s + 1]
        row = jnp.where(v >= 260, 2, jnp.where(v >= 130, 1, 0))
        col = v - 130 * row
        spot = jnp.where(col == 0, 384 + 2 * row, jnp.where(col == 129, 385 + 2 * row, row * 128 + col - 1))
        for j in range(s + 1):
            found[j] = jnp.where((v >= 0) & (count == j), spot, found[j])
        count = count + jnp.where(v >= 0, 1, 0)
    named[...] = jnp.concatenate(found + [zero] * 7, axis=0)
    size = jnp.maximum(count, CLASSES[-1])
    member = jnp.concatenate([jnp.where(size == n, 1.0, 0.0) for n in CLASSES] + [jnp.zeros((3, 128), f32)], axis=0)
    upto = lax.broadcasted_iota(i32, (128, 128), 0) <= lax.broadcasted_iota(i32, (128, 128), 1)
    run = jnp.dot(member.astype(bf16), jnp.where(upto, 1.0, 0.0).astype(bf16), preferred_element_type=f32)
    lane = lax.broadcasted_iota(i32, (1, 256), 1)
    start = jnp.zeros((1, 1), f32)
    place = jnp.zeros((1, 128), f32)
    spans = jnp.where(lane == 12, jnp.where(reach <= LIMIT, 1.0, 0.0), 0.0)
    for c in range(len(CLASSES)):
        fours = jnp.floor((jnp.sum(member[c:c + 1], axis=1, keepdims=True) + 3.0) * 0.25)
        place = place + member[c:c + 1] * (start + run[c:c + 1] - 1.0)
        spans = spans + jnp.where(lane == c, start, 0.0) + jnp.where(lane == len(CLASSES) + c, fours, 0.0)
        start = start + 4.0 * fours
    hit = jnp.where(place.astype(i32) == lax.broadcasted_iota(i32, (256, 128), 0), 1.0, 0.0).astype(bf16)
    tile = lax.broadcasted_iota(i32, (8, 128), 1)
    what = jnp.where(lax.broadcasted_iota(i32, (8, 128), 0) == 0, tile - 128, 0).astype(f32).astype(bf16)
    order = lax.dot_general(what, hit, NT, preferred_element_type=f32)[0:1] + 128.0
    plan[...] = jnp.concatenate([order, spans, jnp.zeros((6, 256), f32)], axis=0).astype(i32)


def exchange(cuts, d, x_ref, nb, vg, vc, xg, xc, cols0, cols1, cols2, feats, plan, named,
             mine, other, x1, x2, yb, ybig, xtab, ctab, yown, named_s, plan_s, tmp_sem,
             loc_sem, s0, r0, s1, r1, s2, r2, s3, r3, sh, rh):
    ev = lax.axis_index("ev")
    cut = lax.axis_index("cuts")
    core = lax.rem(ev, 2)
    x = lax.rem(lax.div(ev, 2), 4)
    yh = lax.div(ev, 8)
    yl = lax.rem(cut, 2)

    def at(y_, x_, c_):
        return (y_ * 8 + x_ * 2 + c_, cut)

    xp, xm, xo = lax.rem(x + 1, 4), lax.rem(x + 3, 4), lax.rem(x + 2, 4)
    twin = at(yh, x, 1 - core)
    right, left = at(yh, xp, core), at(yh, xm, core)
    across = at(1 - yh, x, core)
    beside = (ev, cut + 1 - 2 * yl)
    ahead, behind = cut + 2 - 4 * yl, cut - 2 + 4 * yl
    ok_ahead = (ahead >= 0) & (ahead < cuts)
    ok_behind = (behind >= 0) & (behind < cuts)
    near, far = 2 - 2 * yl, 2 * yl
    rel = [(de, dc) for de in (-1, 1) for dc in (-1, 0, 1)]

    def exists(de, dc):
        ok = (ev + de >= 0) & (ev + de < 16)
        if dc:
            ok = ok & (cut + dc >= 0) & (cut + dc < cuts)
        return ok

    barrier = pltpu.get_barrier_semaphore()
    for dev in (twin, right, left, across, beside):
        pl.semaphore_signal(barrier, inc=1, device_id=dev, device_id_type=MESH)
    expect = 5
    for ok, c in ((ok_ahead, ahead), (ok_behind, behind)):
        @pl.when(ok)
        def _(c=c):
            pl.semaphore_signal(barrier, inc=1, device_id=(ev, c), device_id_type=MESH)
        expect = expect + ok.astype(jnp.int32)
    for de, dc in rel:
        @pl.when(exists(de, dc))
        def _(de=de, dc=dc):
            pl.semaphore_signal(barrier, inc=1, device_id=(ev + de, cut + dc), device_id_type=MESH)
        expect = expect + exists(de, dc).astype(jnp.int32)

    n = len(PIECES)
    rows = [pl.ds(a, b - a) for a, b, _ in PIECES]
    ha = [pl.ds(a, (b - a) // 2) for a, b, _ in PIECES]
    hb = [pl.ds(a + (b - a) // 2, (b - a) // 2) for a, b, _ in PIECES]
    hx = [pl.ds(a // 2, (b - a) // 2) for a, b, _ in PIECES]

    locs = []
    for p in range(n):
        c = pltpu.make_async_copy(d.at[:, :, :, core, rows[p]], mine.at[:, :, :, rows[p]], loc_sem.at[p])
        c.start()
        locs.append(c)
    pl.semaphore_wait(barrier, expect)

    def remote(src, dst, ss, rs, dev, start=True):
        c = pltpu.make_async_remote_copy(src_ref=src, dst_ref=dst, send_sem=ss, recv_sem=rs,
                                         device_id=dev, device_id_type=MESH)
        if start:
            c.start()
        return c

    order = [xo, xp, xm, x]
    c0 = {}
    for p in range(n):
        for i, xx in enumerate(order):
            c0[p, i] = remote(d.at[:, :, xx, 1 - core, rows[p]], other.at[:, :, xx, rows[p]],
                              s0.at[p * 4 + i], r0.at[p * 4 + i], twin)

    def lend(full, part, sem):
        return remote(full.at[1, :, part], full.at[far, :, part], sh.at[sem], rh.at[sem], beside, False)

    def pass_on(full, part, sem):
        return remote(full.at[near, :, part], full.at[far, :, part], sh.at[sem], rh.at[sem], (ev, ahead), False)

    def corners(full, small, base, act):
        for i, (de, dc) in enumerate(rel):
            c = remote(full.at[1, :, pl.ds(120 if de > 0 else 0, 8)], small.at[1 - dc, 0 if de > 0 else 1],
                       sh.at[base + i], rh.at[base + i], (ev + de, cut + dc), False)
            if act == "start":
                pl.when(exists(de, dc))(c.start)
            elif act == "send":
                pl.when(exists(de, dc))(c.wait_send)
            else:
                pl.when(exists(-de, -dc))(c.wait_recv)

    whole = pl.ds(0, 128)
    xg[1] = x_ref[...]
    lend(xg, whole, 12).start()
    corners(xg, xc, 6, "start")

    own = x_ref[...]
    low, high = jnp.min(own, axis=2, keepdims=True), jnp.max(own, axis=2, keepdims=True)
    mid = jnp.broadcast_to(0.5 * high + 0.5 * low, own.shape)
    yown[...] = own - mid
    for g in range(0, 128, 32):
        ctab[g:g + 32] = three(*[mid[k, g:g + 32] for k in range(3)])
        xtab[128 + g:160 + g] = three(*[own[k, g:g + 32] for k in range(3)])
    xtab[390:] = jnp.zeros((10, 8, 128), f32)
    plan_slots(nb[...], plan, named, jnp.max(0.5 * high - 0.5 * low, axis=(0, 1), keepdims=True)[0])
    local = [pltpu.make_async_copy(named, named_s, tmp_sem.at[0]), pltpu.make_async_copy(plan, plan_s, tmp_sem.at[1])]
    for c in local:
        c.start()
    for c in local:
        c.wait()

    def columns(j, _):
        t = jnp.clip(plan_s[0, j], 0, 127)
        for k, c in enumerate((cols0, cols1, cols2)):
            c[j] = jnp.transpose(jnp.broadcast_to(yown[k, pl.ds(t, 1)], (128, 128)))
        return 0

    def features(j, _):
        t = jnp.clip(plan_s[0, j], 0, 127)
        c = ctab[t]
        for s in range(9):
            y = jnp.clip(xtab[jnp.clip(named_s[s, t], 0, 399)] - c, -1e4, 1e4)
            b = y * y
            feats[j * 9 + s] = y * (2 * C2)
            feats[j * 9 + s, 3:4] = (b[0:1] + b[1:2] + b[2:3]) * (-C2) - SHIFT
        return 0

    def some_columns(i):
        lax.fori_loop(18 * i, 18 * i + 18, columns, 0)

    def neighbour_positions():
        pl.when(ok_behind)(pass_on(xg, whole, 13).wait_recv)
        corners(xg, xc, 6, "recv")
        for s in (0, 2):
            for g in range(0, 128, 32):
                xtab[s * 128 + g:s * 128 + g + 32] = three(*[xg[s, k, g:g + 32] for k in range(3)])
        for s in range(3):
            for e, r in ((0, 7), (1, 0)):
                xtab[384 + 2 * s + e:385 + 2 * s + e] = three(*[xc[s, e, k, r:r + 1] for k in range(3)])

    c1, c2, c3 = {}, {}, {}

    def arrive(p, xx, i):
        c0[p, i].wait_recv()
        mine[:, :, xx, rows[p]] += other[:, :, xx, rows[p]]

    def level(p, k):
        first = PIECES[p][2]
        if first:
            ys, step = slice(None), k
        else:
            ys, step = pl.ds(yh, 1), k - 1
        if k == 1:
            locs[p].wait()
            arrive(p, xo, 0)
            if not first:
                for i in (1, 2, 3):
                    arrive(p, order[i], i)
                c3[p] = remote(mine.at[:, 1 - yh, :, rows[p]], ybig.at[:, :, pl.ds(0, PIECES[p][1] - PIECES[p][0])], s3.at[p], r3.at[p], across)
        if k == 2 and not first:
            c3[p].wait_recv()
            mine[:, yh, :, rows[p]] += ybig[:, :, pl.ds(0, PIECES[p][1] - PIECES[p][0])]
        if step == 1:
            for side, half, dev in ((0, ha[p], right), (1, hb[p], left)):
                c1[p, side] = remote(mine.at[:, ys, xo, half], x1.at[side, :, ys, hx[p]], s1.at[2 * p + side], r1.at[2 * p + side], dev)
        elif step == 2:
            for side, xx, half, dev in ((0, xp, ha[p], right), (1, xm, hb[p], left)):
                if first:
                    arrive(p, xx, 1 + side)
                c1[p, side].wait_recv()
                mine[:, ys, xx, half] += x1[side, :, ys, hx[p]]
                c2[p, side] = remote(mine.at[:, ys, xx, rows[p]], x2.at[side, :, ys, rows[p]], s2.at[2 * p + side], r2.at[2 * p + side], dev)
        elif step == 3:
            if first:
                arrive(p, x, 3)
            for side in (0, 1):
                c2[p, side].wait_recv()
                mine[:, ys, x, rows[p]] += x2[side, :, ys, rows[p]]
            if first:
                c3[p] = remote(mine.at[:, 1 - yh, x, rows[p]], yb.at[:, rows[p]], s3.at[p], r3.at[p], across)
            else:
                vg[1, :, rows[p]] = mine[:, yh, x, rows[p]]
                lend(vg, rows[p], 14 + p).start()
        elif step == 4:
            c3[p].wait_recv()
            vg[1, :, rows[p]] = mine[:, yh, x, rows[p]] + yb[:, rows[p]]
            lend(vg, rows[p], 14 + p).start()

    some_columns(0)
    for p in range(n):
        level(p, 1)
    some_columns(1)
    lend(xg, whole, 12).wait_recv()
    pl.when(ok_ahead)(pass_on(xg, whole, 13).start)
    some_columns(2)
    for p in range(n):
        level(p, 2)
    some_columns(3)
    some_columns(4)
    for p in range(n):
        level(p, 3)
    some_columns(5)
    neighbour_positions()
    lax.fori_loop(0, PLACES // 2, features, 0)
    for p in range(n):
        level(p, 4)
    corners(vg, vc, 0, "start")
    lax.fori_loop(PLACES // 2, PLACES, features, 0)
    some_columns(6)
    for p in reversed(range(n)):
        lend(vg, rows[p], 14 + p).wait_recv()
        pl.when(ok_ahead)(pass_on(vg, rows[p], 14 + n + p).start)
    some_columns(7)
    for p in range(n):
        pl.when(ok_behind)(pass_on(vg, rows[p], 14 + n + p).wait_recv)
    corners(vg, vc, 0, "recv")

    for c in list(c0.values()) + list(c1.values()) + list(c2.values()) + list(c3.values()):
        c.wait_send()
    lend(xg, whole, 12).wait_send()
    pl.when(ok_ahead)(pass_on(xg, whole, 13).wait_send)
    for p in range(n):
        lend(vg, rows[p], 14 + p).wait_send()
        pl.when(ok_ahead)(pass_on(vg, rows[p], 14 + n + p).wait_send)
    corners(xg, xc, 6, "send")
    corners(vg, vc, 0, "send")


def run_exchange(kern, coords, nb, cuts):
    n = len(PIECES)
    deep = max(b - a for a, b, first in PIECES if not first)
    vm = pl.BlockSpec(memory_space=pltpu.VMEM)
    dma = pltpu.SemaphoreType.DMA
    shape = jax.ShapeDtypeStruct
    return pl.pallas_call(
        functools.partial(exchange, cuts),
        out_shape=[shape((3, 3, 128, 128), f32), shape((3, 2, 3, 8, 128), f32),
                   shape((3, 3, 128, 128), f32), shape((3, 2, 3, 8, 128), f32),
                   *[shape((PLACES, 128, 128), f32)] * 3, shape((PLACES * 9, 8, 128), f32),
                   shape((8, 256), jnp.int32), shape((16, 128), jnp.int32)],
        in_specs=[pl.BlockSpec(memory_space=pltpu.HBM), vm, vm],
        out_specs=[vm] * 10,
        scratch_shapes=[
            pltpu.VMEM((3, 2, 4, 128, 128), f32), pltpu.VMEM((3, 2, 4, 128, 128), f32),
            pltpu.VMEM((2, 3, 2, 64, 128), f32), pltpu.VMEM((2, 3, 2, 128, 128), f32),
            pltpu.VMEM((3, 128, 128), f32), pltpu.VMEM((3, 4, deep, 128), f32),
            pltpu.VMEM((400, 8, 128), f32), pltpu.VMEM((128, 8, 128), f32), pltpu.VMEM((3, 128, 128), f32),
            pltpu.SMEM((16, 128), jnp.int32), pltpu.SMEM((8, 256), jnp.int32), dma((2,)),
            dma((n,)), dma((4 * n,)), dma((4 * n,)), dma((2 * n,)), dma((2 * n,)), dma((2 * n,)), dma((2 * n,)),
            dma((n,)), dma((n,)), dma((14 + 2 * n,)), dma((14 + 2 * n,))],
        compiler_params=pltpu.CompilerParams(collective_id=0, has_side_effects=True, vmem_limit_bytes=VM1 * 2**20),
        name="event_sum_and_halo",
    )(kern, coords, nb)


def smooth_kernel(plan, named, vg, vc, xg, xc, cols0, cols1, cols2, feats, out, lp, vtab, sm, xtab, pa):
    row8 = lax.broadcasted_iota(jnp.int32, (1, 8, 128), 1)

    def values(at, v):
        n = v.shape[0]
        v = jnp.where(row8 < 3, v, jnp.where(row8 == 3, 1.0, 0.0))
        hi = v.astype(bf16).astype(f32)
        vtab[at:at + n] = jnp.concatenate([hi, v - hi], axis=1).astype(bf16)

    for s in range(3):
        for g in range(0, 128, 32):
            values(s * 128 + g, three(*[vg[s, k, g:g + 32] for k in range(3)]))
        for e, r in ((0, 7), (1, 0)):
            values(384 + 2 * s + e, three(*[vc[s, e, k, r:r + 1] for k in range(3)]))
    vtab[390:] = jnp.zeros((10, 16, 128), bf16)

    def settle(t, r):
        total = r[:, :128] + r[:, 128:]
        mean = (total[0:3] + total[8:11]) / total[3:4]
        for k in range(3):
            sm[k, pl.ds(t, 1)] = mean[k:k + 1]

    def gather(n, t, j):
        tt = jnp.minimum(t, 127)
        col = [c[j] for c in (cols0, cols1, cols2)]
        total = None
        for a in range(0, n, 2):
            both, v = [], []
            for s in range(a, min(a + 2, n)):
                r = [jnp.broadcast_to(feats[j * 9 + s, k:k + 1], (128, 128)) for k in range(4)]
                w = jnp.exp2(((col[0] * r[0] + r[3]) + col[1] * r[1]) + col[2] * r[2])
                hi = w.astype(bf16)
                both.append(jnp.concatenate([hi, (w - hi.astype(f32)).astype(bf16)], axis=0))
                v.append(vtab[named[s, tt]])
            r = lax.dot_general(jnp.concatenate(v, axis=1), jnp.concatenate(both, axis=1), NT, preferred_element_type=f32)
            total = r if total is None else total + r
        return total

    wide = plan[1, 12] == 0

    @pl.when(jnp.logical_not(wide))
    def _():
        for c, n in enumerate(CLASSES):
            first = plan[1, c]

            def body(i, _, n=n, first=first):
                at = first + 4 * i
                t = [plan[0, at + k] for k in range(4)]
                got = [gather(n, t[k], at + k) for k in range(4)]
                for k in range(4):
                    settle(t[k], got[k])
                return 0

            lax.fori_loop(0, plan[1, len(CLASSES) + c], body, 0)

    @pl.when(wide)
    def _():
        for s in range(3):
            for g in range(0, 128, 32):
                xtab[s * 128 + g:s * 128 + g + 32] = three(*[xg[s, k, g:g + 32] for k in range(3)])
            for e, r in ((0, 7), (1, 0)):
                xtab[384 + 2 * s + e:385 + 2 * s + e] = three(*[xc[s, e, k, r:r + 1] for k in range(3)])
        xtab[390:] = jnp.zeros((10, 8, 128), f32)

        def tile(t, _):
            here = xtab[128 + t]
            for a in range(3):
                pa[a] = jnp.transpose(jnp.broadcast_to(here[a:a + 1], (128, 128)))

            def slot(s, total):
                g = named[s, t]
                q = xtab[g]
                dist = jnp.zeros((128, 128), f32)
                for a in range(3):
                    diff = pa[a] - q[a:a + 1]
                    dist = dist + diff * diff
                w = jnp.exp(dist * (-1.0 / 0.72))
                hi = w.astype(bf16)
                both = jnp.concatenate([hi, (w - hi.astype(f32)).astype(bf16)], axis=0)
                return total + lax.dot_general(vtab[g], both, NT, preferred_element_type=f32)

            settle(t, lax.fori_loop(0, 9, slot, jnp.zeros((16, 256), f32)))
            return 0

        lax.fori_loop(0, 128, tile, 0)

    got = sm[:, 0:128]
    out[...] = got
    lp[...] = jnp.sum(jnp.sqrt(got * got + 0.01).reshape(48, 8, 128), axis=0)


def run_smooth(vg, vc, xg, xc, cols0, cols1, cols2, feats, plan, named):
    vm, sm = pl.BlockSpec(memory_space=pltpu.VMEM), pl.BlockSpec(memory_space=pltpu.SMEM)
    return pl.pallas_call(
        smooth_kernel,
        out_shape=[jax.ShapeDtypeStruct((3, 128, 128), f32), jax.ShapeDtypeStruct((8, 128), f32)],
        in_specs=[sm] * 2 + [vm] * 8,
        out_specs=[vm] * 2,
        scratch_shapes=[
            pltpu.VMEM((400, 16, 128), bf16), pltpu.VMEM((3, 136, 128), f32),
            pltpu.VMEM((400, 8, 128), f32), pltpu.VMEM((3, 128, 128), f32)],
        compiler_params=pltpu.CompilerParams(vmem_limit_bytes=VM2 * 2**20),
        name="smooth_tiles",
    )(plan, named, vg, vc, xg, xc, cols0, cols1, cols2, feats)


def total_kernel(cuts, smoothed, part, out, held, ss, rs):
    ev, cut = lax.axis_index("ev"), lax.axis_index("cuts")
    yh, inner = lax.div(ev, 8) * 8, lax.rem(ev, 8)
    steps = [[(yh + lax.rem(inner + d, 8), cut) for d in range(1, 8)]]
    low = min(4, cuts)
    base, lane = lax.div(cut, low) * low, lax.rem(cut, low)
    steps.append([(lax.rem(ev + 8 * a, 16), base + lax.rem(lane + b, low)) for a in (0, 1) for b in range(low) if a + b])
    if cuts > low:
        steps.append([(ev, lax.rem(cut + d * low, cuts)) for d in range(1, cuts // low)])
    barrier = pltpu.get_barrier_semaphore()
    n = 0
    for step in steps:
        for dev in step:
            pl.semaphore_signal(barrier, inc=1, device_id=dev, device_id_type=MESH)
            n += 1
    held[0] = jnp.broadcast_to(jnp.sum(part[...], axis=(0, 1), keepdims=True), (1, 128))
    pl.semaphore_wait(barrier, n)
    got = smoothed[...]
    spread = jnp.sqrt(got * got + 0.01)
    slot, mine, copies = 1, 0, []
    for k, step in enumerate(steps):
        m = len(step)
        for d, dev in enumerate(step):
            c = pltpu.make_async_remote_copy(src_ref=held.at[mine], dst_ref=held.at[slot + d],
                                             send_sem=ss.at[slot + d], recv_sem=rs.at[slot + d], device_id=dev, device_id_type=MESH)
            c.start()
            copies.append(c)
        total = held[mine]
        for d in range(m):
            copies[-m + d].wait_recv()
        for d in range(m):
            total = total + held[slot + d]
        slot += m
        mine = slot
        held[mine] = total
        slot += 1
    everything = 3 * 16384 * 16 * cuts
    out[...] = held[mine, 0:1, 0:1] / everything / spread
    for c in copies:
        c.wait_send()


def run_total(smoothed, part, cuts):
    vm = pl.BlockSpec(memory_space=pltpu.VMEM)
    dma = pltpu.SemaphoreType.DMA
    return pl.pallas_call(
        functools.partial(total_kernel, cuts),
        out_shape=jax.ShapeDtypeStruct((3, 128, 128), f32),
        in_specs=[vm, vm], out_specs=vm,
        scratch_shapes=[pltpu.VMEM((32, 1, 128), f32), dma((32,)), dma((32,))],
        compiler_params=pltpu.CompilerParams(collective_id=1, has_side_effects=True, vmem_limit_bytes=8 * 2**20),
        name="sum_over_devices",
    )(smoothed, part)


def on_device(cuts, kernels, coords, neighbours):
    got = run_exchange(kernels.reshape(3, 2, 4, 2, 128, 128), coords.reshape(3, 128, 128), neighbours[0].T, cuts)
    smoothed, part = run_smooth(*got)
    weights = run_total(smoothed, part, cuts)
    return smoothed.reshape(3, 1, 16384), weights.reshape(3, 1, 16384)


def solution(mesh):
    cuts = mesh.shape["cuts"]
    return jax.shard_map(
        functools.partial(on_device, cuts),
        mesh=mesh,
        in_specs=(P("ev", None, "cuts", None), P(None, "cuts", "ev"), P("cuts", "ev", None)),
        out_specs=(P(None, "cuts", "ev"), P(None, "cuts", "ev")),
        check_vma=False,
    )
```

time: 505 us -> 104 us (0.21)
  waiting for transfers between devices: 189 us -> 0 us
  blocking collectives: 109 us -> 0 us
  matrix products: 98.3 us -> 0 us
  Pallas kernels: 0 us -> 97.7 us
  other arithmetic: 50.9 us -> 0 us
  local copies, waits for them, and re-layouts: 32.1 us -> 5.11 us
  between operations: 14.8 us -> 0.65 us
  starting transfers between devices: 8.24 us -> 0 us
    psum x1 -> x0, waiting for transfers between devices: 171 us -> none  [on_device(): total = lax.psum(local, 'ev')]
    psum x1 -> x0, blocking collectives: 109 us -> none  [on_device(): lp_sum = lax.psum(jnp.sum(spread), ('ev', 'cuts'))]
    dot_general x32 -> x0, matrix products: 98.3 us -> none  [one(): jnp.einsum('tpsq,ktsq->ktp', weights, near[:count], precision=lax.Precisi...]
    pallas_call x0 -> x3, Pallas kernels: none -> 97.7 us  [the longest x1 40.6 us: run_exchange(): pl.pallas_call(functools.partial(exchange, cuts), out_shape=[shape((3, 3,...]
    reduce_sum x33 -> x0, other arithmetic: 44.1 us -> none  [the longest x32 43.3 us: one(): denom = jnp.sum(weights, axis=(2, 3))]
    gather x32 -> x0, local copies, waits for them, and re-layouts: 19 us -> none  [one(): jnp.take(grid, safe.reshape(-1), axis=1)]
    ppermute x4 -> x0, waiting for transfers between devices: 17.6 us -> none  [the longest x2 15.5 us: extended(): lax.ppermute(tail, axis, [(i, (i + 1) % count) for i in range(ends)])]
    ppermute x4 -> x0, starting transfers between devices: 8.2 us -> none  [the longest x2 4.16 us: extended(): lax.ppermute(tail, axis, [(i, (i + 1) % count) for i in range(ends)])]
  transfers between devices with their start and end apart: 5 -> 0, of which waited for: 3 -> 0; matrix products, arithmetic and copies ran while one was open for 0% -> 0% of each run, Pallas kernels for 0% -> 0%
where the time goes in v2:
time: 104 us; the launch traced here: 103 us
  Pallas kernels  97.7 us (94%)
  local copies, waits for them, and re-layouts  5.11 us (5%)
    pallas_call x1, Pallas kernels, run_exchange(): pl.pallas_call(functools.partial(exchange, cuts), out_shape=[shape((3, 3,...  40.6 us
    pallas_call x1, Pallas kernels, run_total(): pl.pallas_call(functools.partial(total_kernel, cuts), out_shape=jax.Shape...  35 us
    pallas_call x1, Pallas kernels, run_smooth(): pl.pallas_call(smooth_kernel, out_shape=[jax.ShapeDtypeStruct((3, 128, 12...  22.1 us
    unnamed x8, local copies, waits for them, and re-layouts  5.11 us

profile of v2, /device:TPU:1, one launch (start us, length us, event | category | flops | bytes accessed | tf_op | source)
XLA Modules:
  0.0 103.5 jit_solution(12153364485688508381)
XLA Ops:
  0.6 0.7 copy.11
  1.3 0.0 copy-start
  1.3 1.9 %copy-done = f32[1,3,1,262144]{3,2,1,0:T(1,128)S(1)} copy-done((f32[1,3,1,262144]{3,2,1,0:T(1,128)S(1)}, f32[1,3,1,262144]{3,2,1,0:T(1,128)}, u32[]{:S(2)}) %copy-start) | copy-done | bytes 3145752
  3.2 0.0 copy-start.1
  3.2 0.9 copy-done.1
  4.1 40.6 %event_sum_and_halo.1 = (f32[3,3,128,128]{3,2,1,0:T(8,128)S(1)}, f32[3,2,3,8,128]{4,3,2,1,0:T(8,128)S(1)}, f32[3,3,128,128]{3,2,1,0:T(8,128)S(1)}, f32[3,2,3,8,1...) custom-call(f32[3,2,4,2,128,128]{5,4,3,2,1,0:T(8,128)S(1)} %bitcast., ...), custom_call_target="tpu_custom_call" | custom-call | tf_op jit(solution)/shard_map/event_sum_and_halo/pallas_call | solution.py:296
  44.7 22.1 %smooth_tiles.1 = (f32[3,128,128]{2,1,0:T(8,128)}, f32[8,128]{1,0:T(8,128)S(1)}) custom-call(s32[8,256]{1,0:T(8,128)S(1)} %get-tuple-element.14.plan, s32[16,128]{1,0:T(8,128)S(1)} %get-tuple-element.15.named, f32[3,3,128,128]{3,2,1,0:T(8,128)S(1)} %get-tuple-element.16.vg, f32[3,2,3,8,128]{4,3,2,1,0:T(8,128)S(1)} %get-tuple-element.17.vc, ...), custom_call_target="tpu_custom_call" | custom-call | tf_op jit(solution)/shard_map/smooth_tiles/pallas_call | solution.py:410
  66.9 0.0 copy-start.2
  66.9 0.9 copy-done.2
  67.8 35.0 %sum_over_devices.1 = f32[3,128,128]{2,1,0:T(8,128)S(1)} custom-call(f32[3,128,128]{2,1,0:T(8,128)S(1)} %copy-done.2, f32[8,128]{1,0:T(8,128)S(1)} %get-tuple-element.25.part), custom_call_target="tpu_custom_call" | custom-call | tf_op jit(solution)/shard_map/sum_over_devices/pallas_call | solution.py:468
  102.8 0.7 copy.13
Async XLA Ops:
  1.3 1.9 %copy-start = (f32[1,3,1,262144]{3,2,1,0:T(1,128)S(1)}, f32[1,3,1,262144]{3,2,1,0:T(1,128)}, u32[]{:S(2)}) copy-start(f32[1,3,1,262144]{3,2,1,0:T(1,128)} %param.3) | copy-start | bytes 9437188
  3.2 0.9 copy-start.1
  66.9 0.9 copy-start.2

commit v3 on v2

--- a/solution.py
+++ b/solution.py
@@ -170,24 +170,29 @@
     for c in local:
         c.wait()
 
-    def columns(j, _):
-        t = jnp.clip(plan_s[0, j], 0, 127)
-        for k, c in enumerate((cols0, cols1, cols2)):
-            c[j] = jnp.transpose(jnp.broadcast_to(yown[k, pl.ds(t, 1)], (128, 128)))
+    def columns(i, _):
+        for j in [6 * i + u for u in range(6)]:
+            t = jnp.clip(plan_s[0, j], 0, 127)
+            for k, c in enumerate((cols0, cols1, cols2)):
+                c[j] = jnp.transpose(jnp.broadcast_to(yown[k, pl.ds(t, 1)], (128, 128)))
         return 0
 
-    def features(j, _):
-        t = jnp.clip(plan_s[0, j], 0, 127)
-        c = ctab[t]
-        for s in range(9):
-            y = jnp.clip(xtab[jnp.clip(named_s[s, t], 0, 399)] - c, -1e4, 1e4)
-            b = y * y
-            feats[j * 9 + s] = y * (2 * C2)
-            feats[j * 9 + s, 3:4] = (b[0:1] + b[1:2] + b[2:3]) * (-C2) - SHIFT
+    def features(i, _):
+        for j in [2 * i + u for u in range(2)]:
+            t = jnp.clip(plan_s[0, j], 0, 127)
+            c = ctab[t]
+            made = []
+            for s in range(9):
+                y = jnp.clip(xtab[jnp.clip(named_s[s, t], 0, 399)] - c, -1e4, 1e4)
+                b = y * y
+                made.append((y * (2 * C2), (b[0:1] + b[1:2] + b[2:3]) * (-C2) - SHIFT))
+            for s, (y, b) in enumerate(made):
+                feats[j * 9 + s] = y
+                feats[j * 9 + s, 3:4] = b
         return 0
 
     def some_columns(i):
-        lax.fori_loop(18 * i, 18 * i + 18, columns, 0)
+        lax.fori_loop(3 * i, 3 * i + 3, columns, 0)
 
     def neighbour_positions():
         pl.when(ok_behind)(pass_on(xg, whole, 13).wait_recv)
@@ -262,11 +267,11 @@
         level(p, 3)
     some_columns(5)
     neighbour_positions()
-    lax.fori_loop(0, PLACES // 2, features, 0)
+    lax.fori_loop(0, PLACES // 4, features, 0)
     for p in range(n):
         level(p, 4)
     corners(vg, vc, 0, "start")
-    lax.fori_loop(PLACES // 2, PLACES, features, 0)
+    lax.fori_loop(PLACES // 4, PLACES // 2, features, 0)
     some_columns(6)
     for p in reversed(range(n)):
         lend(vg, rows[p], 14 + p).wait_recv()
@@ -314,7 +319,7 @@
     )(kern, coords, nb)
 
 
-def smooth_kernel(plan, named, vg, vc, xg, xc, cols0, cols1, cols2, feats, out, lp, vtab, sm, xtab, pa):
+def smooth_kernel(plan, named, vg, vc, xg, xc, cols0, cols1, cols2, feats, out, spread, vtab, sm, xtab, pa):
     row8 = lax.broadcasted_iota(jnp.int32, (1, 8, 128), 1)
 
     def values(at, v):
@@ -402,14 +407,14 @@
 
     got = sm[:, 0:128]
     out[...] = got
-    lp[...] = jnp.sum(jnp.sqrt(got * got + 0.01).reshape(48, 8, 128), axis=0)
+    spread[...] = jnp.sqrt(got * got + 0.01)
 
 
 def run_smooth(vg, vc, xg, xc, cols0, cols1, cols2, feats, plan, named):
     vm, sm = pl.BlockSpec(memory_space=pltpu.VMEM), pl.BlockSpec(memory_space=pltpu.SMEM)
     return pl.pallas_call(
         smooth_kernel,
-        out_shape=[jax.ShapeDtypeStruct((3, 128, 128), f32), jax.ShapeDtypeStruct((8, 128), f32)],
+        out_shape=[jax.ShapeDtypeStruct((3, 128, 128), f32)] * 2,
         in_specs=[sm] * 2 + [vm] * 8,
         out_specs=[vm] * 2,
         scratch_shapes=[
@@ -420,7 +425,7 @@
     )(plan, named, vg, vc, xg, xc, cols0, cols1, cols2, feats)
 
 
-def total_kernel(cuts, smoothed, part, out, held, ss, rs):
+def total_kernel(cuts, spread, out, held, ss, rs):
     ev, cut = lax.axis_index("ev"), lax.axis_index("cuts")
     yh, inner = lax.div(ev, 8) * 8, lax.rem(ev, 8)
     steps = [[(yh + lax.rem(inner + d, 8), cut) for d in range(1, 8)]]
@@ -435,10 +440,9 @@
         for dev in step:
             pl.semaphore_signal(barrier, inc=1, device_id=dev, device_id_type=MESH)
             n += 1
-    held[0] = jnp.broadcast_to(jnp.sum(part[...], axis=(0, 1), keepdims=True), (1, 128))
+    part = jnp.sum(spread[...].reshape(48, 8, 128), axis=0)
+    held[0] = jnp.broadcast_to(jnp.sum(part, axis=(0, 1), keepdims=True), (1, 128))
     pl.semaphore_wait(barrier, n)
-    got = smoothed[...]
-    spread = jnp.sqrt(got * got + 0.01)
     slot, mine, copies = 1, 0, []
     for k, step in enumerate(steps):
         m = len(step)
@@ -457,28 +461,28 @@
         held[mine] = total
         slot += 1
     everything = 3 * 16384 * 16 * cuts
-    out[...] = held[mine, 0:1, 0:1] / everything / spread
+    out[...] = held[mine, 0:1, 0:1] / everything / spread[...]
     for c in copies:
         c.wait_send()
 
 
-def run_total(smoothed, part, cuts):
+def run_total(spread, cuts):
     vm = pl.BlockSpec(memory_space=pltpu.VMEM)
     dma = pltpu.SemaphoreType.DMA
     return pl.pallas_call(
         functools.partial(total_kernel, cuts),
         out_shape=jax.ShapeDtypeStruct((3, 128, 128), f32),
-        in_specs=[vm, vm], out_specs=vm,
+        in_specs=[vm], out_specs=vm,
         scratch_shapes=[pltpu.VMEM((32, 1, 128), f32), dma((32,)), dma((32,))],
         compiler_params=pltpu.CompilerParams(collective_id=1, has_side_effects=True, vmem_limit_bytes=8 * 2**20),
         name="sum_over_devices",
-    )(smoothed, part)
+    )(spread)
 
 
 def on_device(cuts, kernels, coords, neighbours):
     got = run_exchange(kernels.reshape(3, 2, 4, 2, 128, 128), coords.reshape(3, 128, 128), neighbours[0].T, cuts)
-    smoothed, part = run_smooth(*got)
-    weights = run_total(smoothed, part, cuts)
+    smoothed, spread = run_smooth(*got)
+    weights = run_total(spread, cuts)
     return smoothed.reshape(3, 1, 16384), weights.reshape(3, 1, 16384)
 
 

time: 104 us -> 100 us (0.962)
  Pallas kernels: 97.7 us -> 94.8 us
    pallas_call x1, Pallas kernels: 40.6 us -> 35.6 us  [run_exchange(): pl.pallas_call(functools.partial(exchange, cuts), out_shape=[shape((3, 3,...]
    pallas_call x1, Pallas kernels: 35 us -> 37.3 us  [run_total(): pl.pallas_call(functools.partial(total_kernel, cuts), out_shape=jax.Shape...]
    unnamed x8 -> x6, local copies, waits for them, and re-layouts: 5.11 us -> 4.18 us
where the time goes in v3:
time: 100 us; the launch traced here: 99.6 us
  Pallas kernels  94.8 us (95%)
  local copies, waits for them, and re-layouts  4.18 us (4%)
    pallas_call x1, Pallas kernels, run_total(): pl.pallas_call(functools.partial(total_kernel, cuts), out_shape=jax.Shape...  37.3 us
    pallas_call x1, Pallas kernels, run_exchange(): pl.pallas_call(functools.partial(exchange, cuts), out_shape=[shape((3, 3,...  35.6 us
    pallas_call x1, Pallas kernels, run_smooth(): pl.pallas_call(smooth_kernel, out_shape=[jax.ShapeDtypeStruct((3, 128, 12...  21.8 us
    unnamed x6, local copies, waits for them, and re-layouts  4.18 us

profile of v3, /device:TPU:1, one launch (start us, length us, event | category | flops | bytes accessed | tf_op | source)
XLA Modules:
  0.0 99.6 jit_solution(14798058743667173838)
XLA Ops:
  0.6 0.7 copy.11
  1.3 0.0 copy-start
  1.3 1.9 %copy-done = f32[1,3,1,262144]{3,2,1,0:T(1,128)S(1)} copy-done((f32[1,3,1,262144]{3,2,1,0:T(1,128)S(1)}, f32[1,3,1,262144]{3,2,1,0:T(1,128)}, u32[]{:S(2)}) %copy-start) | copy-done | bytes 3145752
  3.2 0.0 copy-start.1
  3.2 0.9 copy-done.1
  4.1 35.6 %event_sum_and_halo.1 = (f32[3,3,128,128]{3,2,1,0:T(8,128)S(1)}, f32[3,2,3,8,128]{4,3,2,1,0:T(8,128)S(1)}, f32[3,3,128,128]{3,2,1,0:T(8,128)S(1)}, f32[3,2,3,8,1...) custom-call(f32[3,2,4,2,128,128]{5,4,3,2,1,0:T(8,128)S(1)} %bitcast., ...), custom_call_target="tpu_custom_call" | custom-call | tf_op jit(solution)/shard_map/event_sum_and_halo/pallas_call | solution.py:301
  39.7 21.8 %smooth_tiles.1 = (f32[3,128,128]{2,1,0:T(8,128)}, f32[3,128,128]{2,1,0:T(8,128)S(1)}) custom-call(s32[8,256]{1,0:T(8,128)S(1)} %get-tuple-element.14.plan, s32[16,128]{1,0:T(8,128)S(1)} %get-tuple-element.15.named, f32[3,3,128,128]{3,2,1,0:T(8,128)S(1)} %get-tuple-element.16.vg, f32[3,2,3,8,128]{4,3,2,1,0:T(8,128)S(1)} %get-tuple-element.17.vc, ...), custom_call_target="tpu_custom_call" | custom-call | tf_op jit(solution)/shard_map/smooth_tiles/pallas_call | solution.py:415
  61.6 37.3 %sum_over_devices.1 = f32[3,128,128]{2,1,0:T(8,128)S(1)} custom-call(f32[3,128,128]{2,1,0:T(8,128)S(1)} %get-tuple-element.25.spread), custom_call_target="tpu_custom_call" | custom-call | tf_op jit(solution)/shard_map/sum_over_devices/pallas_call | solution.py:472
  98.9 0.7 copy.13
Async XLA Ops:
  1.3 1.9 %copy-start = (f32[1,3,1,262144]{3,2,1,0:T(1,128)S(1)}, f32[1,3,1,262144]{3,2,1,0:T(1,128)}, u32[]{:S(2)}) copy-start(f32[1,3,1,262144]{3,2,1,0:T(1,128)} %param.3) | copy-start | bytes 9437188
  3.2 0.9 copy-start.1

commit v4 on v3

--- a/solution.py
+++ b/solution.py
@@ -271,12 +271,12 @@
     for p in range(n):
         level(p, 4)
     corners(vg, vc, 0, "start")
-    lax.fori_loop(PLACES // 4, PLACES // 2, features, 0)
     some_columns(6)
+    some_columns(7)
     for p in reversed(range(n)):
         lend(vg, rows[p], 14 + p).wait_recv()
         pl.when(ok_ahead)(pass_on(vg, rows[p], 14 + n + p).start)
-    some_columns(7)
+    lax.fori_loop(PLACES // 4, PLACES // 2, features, 0)
     for p in range(n):
         pl.when(ok_behind)(pass_on(vg, rows[p], 14 + n + p).wait_recv)
     corners(vg, vc, 0, "recv")

time: 100 us -> 100 us (level)
    pallas_call x1, Pallas kernels: 35.6 us -> 33.8 us  [run_exchange(): pl.pallas_call(functools.partial(exchange, cuts), out_shape=[shape((3, 3,...]
where the time goes in v4:
time: 100 us; the launch traced here: 99.4 us
  Pallas kernels  94.6 us (95%)
  local copies, waits for them, and re-layouts  4.18 us (4%)
    pallas_call x1, Pallas kernels, run_total(): pl.pallas_call(functools.partial(total_kernel, cuts), out_shape=jax.Shape...  38.3 us
    pallas_call x1, Pallas kernels, run_exchange(): pl.pallas_call(functools.partial(exchange, cuts), out_shape=[shape((3, 3,...  33.8 us
    pallas_call x1, Pallas kernels, run_smooth(): pl.pallas_call(smooth_kernel, out_shape=[jax.ShapeDtypeStruct((3, 128, 12...  22.5 us
    unnamed x6, local copies, waits for them, and re-layouts  4.18 us

profile of v4, /device:TPU:1, one launch (start us, length us, event | category | flops | bytes accessed | tf_op | source)
XLA Modules:
  0.0 99.4 jit_solution(2555487265863596458)
XLA Ops:
  0.6 0.7 copy.11
  1.3 0.0 copy-start
  1.3 1.9 %copy-done = f32[1,3,1,262144]{3,2,1,0:T(1,128)S(1)} copy-done((f32[1,3,1,262144]{3,2,1,0:T(1,128)S(1)}, f32[1,3,1,262144]{3,2,1,0:T(1,128)}, u32[]{:S(2)}) %copy-start) | copy-done | bytes 3145752
  3.2 0.0 copy-start.1
  3.2 0.9 copy-done.1
  4.1 33.8 %event_sum_and_halo.1 = (f32[3,3,128,128]{3,2,1,0:T(8,128)S(1)}, f32[3,2,3,8,128]{4,3,2,1,0:T(8,128)S(1)}, f32[3,3,128,128]{3,2,1,0:T(8,128)S(1)}, f32[3,2,3,8,1...) custom-call(f32[3,2,4,2,128,128]{5,4,3,2,1,0:T(8,128)S(1)} %bitcast., ...), custom_call_target="tpu_custom_call" | custom-call | tf_op jit(solution)/shard_map/event_sum_and_halo/pallas_call | solution.py:301
  38.0 22.5 %smooth_tiles.1 = (f32[3,128,128]{2,1,0:T(8,128)}, f32[3,128,128]{2,1,0:T(8,128)S(1)}) custom-call(s32[8,256]{1,0:T(8,128)S(1)} %get-tuple-element.14.plan, s32[16,128]{1,0:T(8,128)S(1)} %get-tuple-element.15.named, f32[3,3,128,128]{3,2,1,0:T(8,128)S(1)} %get-tuple-element.16.vg, f32[3,2,3,8,128]{4,3,2,1,0:T(8,128)S(1)} %get-tuple-element.17.vc, ...), custom_call_target="tpu_custom_call" | custom-call | tf_op jit(solution)/shard_map/smooth_tiles/pallas_call | solution.py:415
  60.5 38.3 %sum_over_devices.1 = f32[3,128,128]{2,1,0:T(8,128)S(1)} custom-call(f32[3,128,128]{2,1,0:T(8,128)S(1)} %get-tuple-element.25.spread), custom_call_target="tpu_custom_call" | custom-call | tf_op jit(solution)/shard_map/sum_over_devices/pallas_call | solution.py:472
  98.8 0.7 copy.13
Async XLA Ops:
  1.3 1.9 %copy-start = (f32[1,3,1,262144]{3,2,1,0:T(1,128)S(1)}, f32[1,3,1,262144]{3,2,1,0:T(1,128)}, u32[]{:S(2)}) copy-start(f32[1,3,1,262144]{3,2,1,0:T(1,128)} %param.3) | copy-start | bytes 9437188
  3.2 0.9 copy-start.1
